TPU v7x, 256 devices: a whole 4x4x8 slice. The times are simulated.
256 devices in a mesh: row: 8 (over z), col: 32 (over x, y, core).
Axes of the slice: x: 4, y: 4, z: 8, core: 2. Of those that a mesh axis runs over, the one named last changes fastest.
Arguments:
- xn: bfloat16 [1024, 2048], P('col', 'row'), may hold values from -6 to 6
- w_qkv: bfloat16 [2048, 6144], P('row', 'col'), may hold values from -0.125 to 0.125
- w_out: bfloat16 [2048, 2048], P('col', 'row'), may hold values from -0.125 to 0.125
- pool: bfloat16 [2048, 64, 4096], P('row', None, 'col'), may hold values from -136 to 136
- page_table: int32 [1024, 64], P('row'), may hold values from 0 to 271
- lengths: int32 [1024], P('row'), may hold values from 1 to 4096, 98304 in all
- mig_src: int32 [128], replicated, may hold values from 0 to 2047, as said below
- deal: int32 [1024], replicated, may hold values from 0 to 1023, each once
Outputs:
- attended: bfloat16 [1024, 2048], P('col', 'row')
- landed: bfloat16 [128, 64, 4096], P('row', None, 'col')
Inputs may be any that keep to these rules, and one draw needn't show every extreme that they name: `page_table`: page ids of a request refer to its own row block: below 256 its pool pages, from 256 its landing slots. `lengths`: the longest request has exactly 4096 cache tokens. `mig_src`: slot d belongs to row block d // 16; its source page lies in the pool pages of another row block. `deal`: a permutation of the requests.
All inputs are finite; a program needn't handle non-finite values. No bound on the sum of `lengths` on one device may be relied on, other than what follows from the above.
Results may differ from a plain program's by a relative error of at most 0.02.
Values may be sent and summed in bfloat16 or wider, within the bound.
A program may use at most 128 MiB of HBM per device.

v0:
```python
import jax
import jax.numpy as jnp
from jax import lax
from jax.sharding import PartitionSpec as P

HEAD_DIM = 64
PAGE = 64
theta_base = 130000.0
neg_large = -1e30


def rotate(values, positions):
    half = values.shape[-1] // 2
    freqs = theta_base ** (-(jnp.arange(half, dtype=jnp.float32) * 2.0 / values.shape[-1]))
    angles = positions.astype(jnp.float32)[:, None, None] * freqs[None, None, :]
    cosine = jnp.cos(angles)
    sine = jnp.sin(angles)
    first = values[..., :half]
    second = values[..., half:]
    return jnp.concatenate(
        [first * cosine - second * sine, second * cosine + first * sine], axis=-1
    )


def attend(query, key_new, value_new, table, lens, key_pool, value_pool):
    req_count = query.shape[0]
    heads_here = query.shape[1]
    pages_all = table.shape[1]
    pages_block = min(pages_all, max(1, 512 // PAGE))
    block_len = pages_block * PAGE
    longest = jnp.max(lens)
    block_count = (longest + block_len - 1) // block_len
    positions = jnp.arange(block_len, dtype=jnp.int32)

    def score_block(block_no, scores):
        page_ids = lax.dynamic_slice_in_dim(table, block_no * pages_block, pages_block, 1)
        keys = key_pool[page_ids].reshape(req_count, block_len, heads_here, HEAD_DIM)
        block_scores = (
            jnp.einsum("rhe,rthe->rht", query, keys, preferred_element_type=jnp.float32) * 0.125
        )
        valid = (block_no * block_len + positions)[None, None, :] < lens[:, None, None]
        block_scores = jnp.where(valid, block_scores, neg_large)
        return lax.dynamic_update_slice_in_dim(scores, block_scores, block_no * block_len, 2)

    initial = jnp.full((req_count, heads_here, pages_all * PAGE), neg_large, jnp.float32)
    scores = lax.fori_loop(0, block_count, score_block, initial)
    score_new = jnp.sum(query.astype(jnp.float32) * key_new.astype(jnp.float32), axis=-1) * 0.125
    top = jnp.maximum(jnp.max(scores, axis=2), score_new)
    expo_new = jnp.exp(score_new - top)
    total = jnp.sum(jnp.exp(scores - top[..., None]), axis=2) + expo_new

    def value_block(block_no, numer):
        block_scores = lax.dynamic_slice_in_dim(scores, block_no * block_len, block_len, 2)
        weights = jnp.exp(block_scores - top[..., None]).astype(jnp.bfloat16)
        page_ids = lax.dynamic_slice_in_dim(table, block_no * pages_block, pages_block, 1)
        values = value_pool[page_ids].reshape(req_count, block_len, heads_here, HEAD_DIM)
        return numer + jnp.einsum(
            "rht,rthe->rhe", weights, values, preferred_element_type=jnp.float32
        )

    numer = lax.fori_loop(
        0, block_count, value_block, jnp.zeros((req_count, heads_here, HEAD_DIM), jnp.float32)
    )
    weight_new = lax.optimization_barrier(expo_new.astype(jnp.bfloat16)).astype(jnp.float32)
    numer = numer + weight_new[..., None] * value_new.astype(jnp.float32)
    return (numer / total[..., None]).astype(jnp.bfloat16)


def on_device(xn, w_qkv, w_out, pool, page_table, lengths, mig_src, deal):
    heads_here = w_out.shape[0] // HEAD_DIM
    rows_all = xn.shape[0] * lax.axis_size("col")
    row_count = lax.axis_size("row")
    req_row = rows_all // row_count
    inverse = jnp.zeros((rows_all,), jnp.int32).at[deal].set(jnp.arange(rows_all, dtype=jnp.int32))
    gathered = lax.all_gather(xn, "col", axis=0, tiled=True)
    chosen = inverse
    projected = lax.psum_scatter(
        jnp.dot(jnp.take(gathered, chosen, axis=0), w_qkv, preferred_element_type=jnp.float32),
        "row",
        scatter_dimension=0,
        tiled=True,
    )
    projected = projected.reshape(req_row, heads_here, 3, HEAD_DIM)
    query = rotate(projected[:, :, 0], lengths).astype(jnp.bfloat16)
    key_new = rotate(projected[:, :, 1], lengths).astype(jnp.bfloat16)
    value_new = projected[:, :, 2].astype(jnp.bfloat16)
    my_row = lax.axis_index("row")
    pool_dev = pool.shape[0]
    land_dev = mig_src.shape[0] // row_count
    source_row = mig_src // pool_dev
    local_page = jnp.clip(mig_src - my_row * pool_dev, 0, pool_dev - 1)
    outgoing = jnp.where(
        (source_row == my_row)[:, None, None],
        jnp.take(pool, local_page, axis=0),
        jnp.zeros((), jnp.bfloat16),
    )
    outgoing = outgoing.reshape(row_count, land_dev, pool.shape[1], pool.shape[2])
    received = lax.all_to_all(outgoing, "row", split_axis=0, concat_axis=0, tiled=True)
    my_sources = lax.dynamic_slice_in_dim(source_row, my_row * land_dev, land_dev)
    landed = received[my_sources, jnp.arange(land_dev)]
    combined = jnp.concatenate([pool, landed], axis=0)
    combined = combined.reshape(combined.shape[0], PAGE, heads_here, 2, HEAD_DIM)
    key_pool = combined[:, :, :, 0]
    value_pool = combined[:, :, :, 1]
    mixed = attend(query, key_new, value_new, page_table, lengths, key_pool, value_pool)
    mixed = mixed.reshape(req_row, heads_here * HEAD_DIM)
    mixed_all = lax.all_gather(mixed, "row", axis=0, tiled=True)
    chosen = deal
    attended = lax.psum_scatter(
        jnp.dot(
            jnp.take(mixed_all, chosen, axis=0), w_out, preferred_element_type=jnp.float32
        ).astype(jnp.bfloat16),
        "col",
        scatter_dimension=0,
        tiled=True,
    )
    return (attended, landed)


def solution(mesh):
    placed = (
        P("col", "row"),
        P("row", "col"),
        P("col", "row"),
        P("row", None, "col"),
        P("row", None),
        P("row"),
        P(),
        P(),
    )
    return jax.shard_map(
        on_device,
        mesh=mesh,
        in_specs=placed,
        out_specs=(P("col", "row"), P("row", None, "col")),
        check_vma=False,
    )
```

profile of v0, /device:TPU:2, one launch (start us, length us, event | category | flops | bytes accessed | tf_op | source)
XLA Modules:
  0.0 795.2 jit_solution(766521219525709486)
XLA Ops:
  26.3 24.8 %all_gather.6 = bf16[1024,256]{1,0:T(8,128)(2,1)S(1)} all-gather(bf16[32,256]{1,0:T(8,128)(2,1)S(1)} %copy-done.6), channel_id=1, replica_groups=mesh['row'=8,'col'=32] {'col'}, dimensions={0}, use_global_device_ids=true | all-gather | bytes 540672 | tf_op jit(solution)/shard_map/all_gather | solution.py:75
  65.5 28.8 %reduce-scatter.3.cloned.1.call-done = f32[128,192]{0,1:T(8,128)} async-done(((f32[1024,192]{0,1:T(8,128)}), f32[128,192]{0,1:T(8,128)}) %reduce-scatter.3.cloned.1.call-update) | async-done | bytes 98320 | tf_op jit(solution)/shard_map/reduce_scatter | solution.py:77
  106.2 261.0 %while.22 = (s32[]{:T(128)}, f32[128,1,4096]{2,1,0:T(1,128)}, s32[]{:T(128)}, s32[128]{0:T(128)S(1)}, s32[128,64]{1,0:T(8,128)S(1)}, /*index=5*/bf16[272,64,1,64...) while((s32[]{:T(128)}, f32[128,1,4096]{2,1,0:T(1,128)}, ...), condition=%wide.region_4.5_spmd.clone, body=%wide.region_3.4_spmd.clone.sunk | while | flops 8589834 | bytes 31015652 | solution.py:46
  116.2 15.7 %gather_fusion.1 = bf16[1024,64,64]{2,1,0:T(8,128)(2,1)} fusion(bf16[272,64,64]{2,1,0:T(8,128)(2,1)} %copy.78, s32[1024]{0:T(1024)S(1)} %broadcast_clamp_fusion.6), kind=kCustom, calls=%fused_computation.clone.clone.1 | custom fusion | bytes 16781312 | tf_op jit(solution)/shard_map/while/body/gather | solution.py:37
  153.5 15.7 %gather_fusion.1 = bf16[1024,64,64]{2,1,0:T(8,128)(2,1)} fusion(bf16[272,64,64]{2,1,0:T(8,128)(2,1)} %copy.78, s32[1024]{0:T(1024)S(1)} %broadcast_clamp_fusion.6), kind=kCustom, calls=%fused_computation.clone.clone.1 | custom fusion | bytes 16781312 | tf_op jit(solution)/shard_map/while/body/gather | solution.py:37
  181.0 9.9 %copy.78 = bf16[272,64,64]{2,1,0:T(8,128)(2,1)} copy(bf16[272,64,64]{0,2,1:T(8,128)(2,1)} %bitcast.89) | data formatting | bytes 4456448 | tf_op jit(solution)/shard_map
  190.8 15.7 %gather_fusion.1 = bf16[1024,64,64]{2,1,0:T(8,128)(2,1)} fusion(bf16[272,64,64]{2,1,0:T(8,128)(2,1)} %copy.78, s32[1024]{0:T(1024)S(1)} %broadcast_clamp_fusion.6), kind=kCustom, calls=%fused_computation.clone.clone.1 | custom fusion | bytes 16781312 | tf_op jit(solution)/shard_map/while/body/gather | solution.py:37
  228.1 15.7 %gather_fusion.1 = bf16[1024,64,64]{2,1,0:T(8,128)(2,1)} fusion(bf16[272,64,64]{2,1,0:T(8,128)(2,1)} %copy.78, s32[1024]{0:T(1024)S(1)} %broadcast_clamp_fusion.6), kind=kCustom, calls=%fused_computation.clone.clone.1 | custom fusion | bytes 16781312 | tf_op jit(solution)/shard_map/while/body/gather | solution.py:37
  255.6 9.9 %copy.78 = bf16[272,64,64]{2,1,0:T(8,128)(2,1)} copy(bf16[272,64,64]{0,2,1:T(8,128)(2,1)} %bitcast.89) | data formatting | bytes 4456448 | tf_op jit(solution)/shard_map
  265.4 15.7 %gather_fusion.1 = bf16[1024,64,64]{2,1,0:T(8,128)(2,1)} fusion(bf16[272,64,64]{2,1,0:T(8,128)(2,1)} %copy.78, s32[1024]{0:T(1024)S(1)} %broadcast_clamp_fusion.6), kind=kCustom, calls=%fused_computation.clone.clone.1 | custom fusion | bytes 16781312 | tf_op jit(solution)/shard_map/while/body/gather | solution.py:37
  292.8 9.9 %copy.78 = bf16[272,64,64]{2,1,0:T(8,128)(2,1)} copy(bf16[272,64,64]{0,2,1:T(8,128)(2,1)} %bitcast.89) | data formatting | bytes 4456448 | tf_op jit(solution)/shard_map
  302.7 15.7 %gather_fusion.1 = bf16[1024,64,64]{2,1,0:T(8,128)(2,1)} fusion(bf16[272,64,64]{2,1,0:T(8,128)(2,1)} %copy.78, s32[1024]{0:T(1024)S(1)} %broadcast_clamp_fusion.6), kind=kCustom, calls=%fused_computation.clone.clone.1 | custom fusion | bytes 16781312 | tf_op jit(solution)/shard_map/while/body/gather | solution.py:37
  330.1 9.9 %copy.78 = bf16[272,64,64]{2,1,0:T(8,128)(2,1)} copy(bf16[272,64,64]{0,2,1:T(8,128)(2,1)} %bitcast.89) | data formatting | bytes 4456448 | tf_op jit(solution)/shard_map
  340.0 15.7 %gather_fusion.1 = bf16[1024,64,64]{2,1,0:T(8,128)(2,1)} fusion(bf16[272,64,64]{2,1,0:T(8,128)(2,1)} %copy.78, s32[1024]{0:T(1024)S(1)} %broadcast_clamp_fusion.6), kind=kCustom, calls=%fused_computation.clone.clone.1 | custom fusion | bytes 16781312 | tf_op jit(solution)/shard_map/while/body/gather | solution.py:37
  375.0 232.9 %while.21 = (s32[]{:T(128)}, f32[128,1,64]{2,1,0:T(1,128)S(1)}, s32[]{:T(128)}, f32[128,1,4096]{2,1,0:T(1,128)}, f32[128,1]{0,1:T(1,128)S(1)}, /*index=5*/s32[12...) while((s32[]{:T(128)}, f32[128,1,64]{2,1,0:T(1,128)S(1)}, ...), condition=%wide.region_8.9_spmd, body=%wide.region_7.8_spmd.sunk | while | flops 8531978 | bytes 30765792 | solution.py:61
  384.4 15.7 %gather_fusion = bf16[1024,64,64]{2,1,0:T(8,128)(2,1)} fusion(bf16[272,64,64]{2,1,0:T(8,128)(2,1)} %copy.76, s32[1024]{0:T(1024)S(1)} %broadcast_clamp_fusion.5), kind=kCustom, calls=%fused_computation.1.clone.1 | custom fusion | bytes 16781312 | tf_op jit(solution)/shard_map/while/body/gather | solution.py:56
  417.7 15.7 %gather_fusion = bf16[1024,64,64]{2,1,0:T(8,128)(2,1)} fusion(bf16[272,64,64]{2,1,0:T(8,128)(2,1)} %copy.76, s32[1024]{0:T(1024)S(1)} %broadcast_clamp_fusion.5), kind=kCustom, calls=%fused_computation.1.clone.1 | custom fusion | bytes 16781312 | tf_op jit(solution)/shard_map/while/body/gather | solution.py:56
  450.9 15.7 %gather_fusion = bf16[1024,64,64]{2,1,0:T(8,128)(2,1)} fusion(bf16[272,64,64]{2,1,0:T(8,128)(2,1)} %copy.76, s32[1024]{0:T(1024)S(1)} %broadcast_clamp_fusion.5), kind=kCustom, calls=%fused_computation.1.clone.1 | custom fusion | bytes 16781312 | tf_op jit(solution)/shard_map/while/body/gather | solution.py:56
  484.2 15.7 %gather_fusion = bf16[1024,64,64]{2,1,0:T(8,128)(2,1)} fusion(bf16[272,64,64]{2,1,0:T(8,128)(2,1)} %copy.76, s32[1024]{0:T(1024)S(1)} %broadcast_clamp_fusion.5), kind=kCustom, calls=%fused_computation.1.clone.1 | custom fusion | bytes 16781312 | tf_op jit(solution)/shard_map/while/body/gather | solution.py:56
  517.5 15.7 %gather_fusion = bf16[1024,64,64]{2,1,0:T(8,128)(2,1)} fusion(bf16[272,64,64]{2,1,0:T(8,128)(2,1)} %copy.76, s32[1024]{0:T(1024)S(1)} %broadcast_clamp_fusion.5), kind=kCustom, calls=%fused_computation.1.clone.1 | custom fusion | bytes 16781312 | tf_op jit(solution)/shard_map/while/body/gather | solution.py:56
  550.7 15.7 %gather_fusion = bf16[1024,64,64]{2,1,0:T(8,128)(2,1)} fusion(bf16[272,64,64]{2,1,0:T(8,128)(2,1)} %copy.76, s32[1024]{0:T(1024)S(1)} %broadcast_clamp_fusion.5), kind=kCustom, calls=%fused_computation.1.clone.1 | custom fusion | bytes 16781312 | tf_op jit(solution)/shard_map/while/body/gather | solution.py:56
  584.0 15.7 %gather_fusion = bf16[1024,64,64]{2,1,0:T(8,128)(2,1)} fusion(bf16[272,64,64]{2,1,0:T(8,128)(2,1)} %copy.76, s32[1024]{0:T(1024)S(1)} %broadcast_clamp_fusion.5), kind=kCustom, calls=%fused_computation.1.clone.1 | custom fusion | bytes 16781312 | tf_op jit(solution)/shard_map/while/body/gather | solution.py:56
  608.8 92.1 %all-gather = bf16[1024,1,64]{0,2,1:T(8,128)(2,1)S(1)} all-gather(bf16[128,1,64]{0,2,1:T(8,128)(2,1)S(1)} %fusion.16), channel_id=2, replica_groups=mesh['row'=8,'col'=32] {'row'}, dimensions={0}, use_global_device_ids=true | all-gather | bytes 147456 | tf_op jit(solution)/shard_map/all_gather | solution.py:107
  705.5 82.8 %reduce-scatter.5.cloned.1.call-done = bf16[32,256]{1,0:T(8,128)(2,1)} async-done(((bf16[1024,256]{1,0:T(8,128)(2,1)}), bf16[32,256]{1,0:T(8,128)(2,1)}) %reduce-scatter.5.cloned.1.call-update) | async-done | bytes 16400 | tf_op jit(solution)/shard_map/reduce_scatter | solution.py:109
  (174 shorter events, 291.4 us)
Async XLA Ops:
  7.2 47.9 %copy-start = (bf16[256,192]{0,1:T(8,128)(2,1)S(1)}, bf16[256,192]{0,1:T(8,128)(2,1)}, u32[]{:S(2)}) copy-start(bf16[256,192]{0,1:T(8,128)(2,1)} %param.13) | copy-start | bytes 294916
  11.2 10.1 %copy-start.7 = (s32[1024]{0:T(1024)S(1)}, s32[1024]{0:T(1024)}, u32[]{:S(2)}) copy-start(s32[1024]{0:T(1024)} %param.19) | copy-start | bytes 12292
  11.2 15.0 %copy-start.6 = (bf16[32,256]{1,0:T(8,128)(2,1)S(1)}, bf16[32,256]{1,0:T(8,128)(2,1)}, u32[]{:S(2)}) copy-start(bf16[32,256]{1,0:T(8,128)(2,1)} %param.12) | copy-start | bytes 49156
  12.8 82.4 %all-to-all-start = ((bf16[8,16,64,128]{3,2,1,0:T(8,128)(2,1)}), bf16[8,16,64,128]{3,2,1,0:T(8,128)(2,1)S(1)}, u32[]{:S(2)}, u32[]{:S(2)}) async-start(bf16[8,16,64,128]{3,2,1,0:T(8,128)(2,1)} %select_select_fusion), calls=%async_computation | async-start | bytes 4194304 | tf_op jit(solution)/shard_map/all_to_all | solution.py:98
  21.3 35.2 %copy-start.8 = (s32[128]{0:T(128)S(1)}, s32[128]{0:T(128)}, u32[]{:S(2)}) copy-start(s32[128]{0:T(128)} %param.17) | copy-start | bytes 1540
  21.3 72.9 %reduce-scatter.3.cloned.1.call-start = ((), (), s32[]{:S(2)}) async-start(), calls=%async_computation.3 | async-start | bytes 884736 | tf_op jit(solution)/shard_map/reduce_scatter | solution.py:77
  56.4 731.9 %reduce-scatter.5.cloned.1.call-start = ((), (), s32[]{:S(2)}) async-start(), calls=%async_computation.4 | async-start | bytes 540672 | tf_op jit(solution)/shard_map/reduce_scatter | solution.py:109
  57.7 6.9 copy-start.3
  95.8 4.4 copy-start.2
  375.0 326.1 %copy-start.5 = (s32[1024]{0:T(1024)S(1)}, s32[1024]{0:T(1024)}, u32[]{:S(2)}) copy-start(s32[1024]{0:T(1024)} %get-tuple-element.191) | copy-start | bytes 12292
  375.0 329.3 %copy-start.4 = (bf16[64,256]{1,0:T(8,128)(2,1)S(1)}, bf16[64,256]{1,0:T(8,128)(2,1)}, u32[]{:S(2)}) copy-start(bf16[64,256]{1,0:T(8,128)(2,1)} %param.14) | copy-start | bytes 98308
  375.0 329.3 %copy-start.9 = (pred[1024]{0:T(1024)(128)(4,1)S(1)}, pred[1024]{0:T(1024)(128)(4,1)}, u32[]{:S(2)}) copy-start(pred[1024]{0:T(1024)(128)(4,1)} %compare_and_fusion.1) | copy-start | bytes 3076
  607.9 180.4 %copy-start.1 = (bf16[256,192]{0,1:T(8,128)(2,1)S(1)}, bf16[256,192]{0,1:T(8,128)(2,1)}, u32[]{:S(2)}) copy-start(bf16[256,192]{0,1:T(8,128)(2,1)} %param.13) | copy-start | bytes 294916
Sparse Core Ops, SparseCore 0:
  56.5 37.6 reduce-scatter.2
  705.6 82.6 reduce-scatter.4
where the time goes:
time: 798 us; the launch traced here: 795 us
  local copies, waits for them, and re-layouts  410 us (51%)
  blocking collectives  117 us (15%)
  waiting for transfers between devices  112 us (14%)
  matrix products  108 us (14%)
  other arithmetic  23.8 us (3%)
  between operations  15 us (2%)
  starting transfers between devices  8.55 us (1%)
    another operation x21, local copies, waits for them, and re-layouts  138 us
    gather x7, local copies, waits for them, and re-layouts, score_block(): key_pool[page_ids].reshape(req_count, block_len, heads_here, HEAD_DIM)  110 us
    gather x7, local copies, waits for them, and re-layouts, value_block(): value_pool[page_ids].reshape(req_count, block_len, heads_here, HEAD_DIM)  110 us
    all_gather x1, blocking collectives, on_device(): mixed_all = lax.all_gather(mixed, 'row', axis=0, tiled=True)  92.1 us
    reduce_scatter x1, waiting for transfers between devices, on_device(): lax.psum_scatter(jnp.dot(jnp.take(mixed_all, chosen, axis=0), w_out, pref...  82.8 us
    dot_general x7, matrix products, score_block(): jnp.einsum('rhe,rthe->rht', query, keys, preferred_element_type=jnp.float32)  56.5 us
    dot_general x7, matrix products, value_block(): jnp.einsum('rht,rthe->rhe', weights, values, preferred_element_type=jnp.f...  49.4 us
    reduce_scatter x1, waiting for transfers between devices, on_device(): lax.psum_scatter(jnp.dot(jnp.take(gathered, chosen, axis=0), w_qkv, prefe...  28.8 us
  transfers between devices with their start and end apart: 3, of which 2 were waited for; matrix products, arithmetic and copies ran while one was open for 2% of the time, Pallas kernels for 0%

commit v1 on v0

--- a/solution.py
+++ b/solution.py
@@ -72,7 +72,9 @@
     row_count = lax.axis_size("row")
     req_row = rows_all // row_count
     inverse = jnp.zeros((rows_all,), jnp.int32).at[deal].set(jnp.arange(rows_all, dtype=jnp.int32))
-    gathered = lax.all_gather(xn, "col", axis=0, tiled=True)
+    gathered = jnp.concatenate(
+        lax.all_to_all(jnp.stack([xn] * lax.axis_size("col")), "col", 0, 0), axis=0
+    )
     chosen = inverse
     projected = lax.psum_scatter(
         jnp.dot(jnp.take(gathered, chosen, axis=0), w_qkv, preferred_element_type=jnp.float32),

time: 798 us -> 797 us (level)
  blocking collectives: 117 us -> 92.9 us
  waiting for transfers between devices: 112 us -> 125 us
    all_gather x1 -> x0, blocking collectives: 24.8 us -> none  [on_device(): gathered = lax.all_gather(xn, 'col', axis=0, tiled=True)]
    reduce_scatter x1, waiting for transfers between devices: 28.8 us -> 38.9 us  [on_device(): lax.psum_scatter(jnp.dot(jnp.take(gathered, chosen, axis=0), w_qkv, prefe...]
    another operation x21 -> x22, local copies, waits for them, and re-layouts: 138 us -> 140 us
  transfers between devices with their start and end apart: 3 -> 4, of which waited for: 2 -> 3; matrix products, arithmetic and copies ran while one was open for 2% -> 3% of each run, Pallas kernels for 0% -> 0%
where the time goes in v1:
time: 797 us; the launch traced here: 793 us
  local copies, waits for them, and re-layouts  412 us (52%)
  waiting for transfers between devices  125 us (16%)
  matrix products  108 us (14%)
  blocking collectives  92.9 us (12%)
  other arithmetic  23.8 us (3%)
  starting transfers between devices  16.2 us (2%)
  between operations  15 us (2%)
    another operation x21, local copies, waits for them, and re-layouts  138 us
    gather x7, local copies, waits for them, and re-layouts, score_block(): key_pool[page_ids].reshape(req_count, block_len, heads_here, HEAD_DIM)  110 us
    gather x7, local copies, waits for them, and re-layouts, value_block(): value_pool[page_ids].reshape(req_count, block_len, heads_here, HEAD_DIM)  110 us
    all_gather x1, blocking collectives, on_device(): mixed_all = lax.all_gather(mixed, 'row', axis=0, tiled=True)  92.9 us
    reduce_scatter x1, waiting for transfers between devices, on_device(): lax.psum_scatter(jnp.dot(jnp.take(mixed_all, chosen, axis=0), w_out, pref...  81.9 us
    dot_general x7, matrix products, score_block(): jnp.einsum('rhe,rthe->rht', query, keys, preferred_element_type=jnp.float32)  56.5 us
    dot_general x7, matrix products, value_block(): jnp.einsum('rht,rthe->rhe', weights, values, preferred_element_type=jnp.f...  49.4 us
    reduce_scatter x1, waiting for transfers between devices, on_device(): lax.psum_scatter(jnp.dot(jnp.take(gathered, chosen, axis=0), w_qkv, prefe...  38.9 us
  transfers between devices with their start and end apart: 4, of which 3 were waited for; matrix products, arithmetic and copies ran while one was open for 3% of the time, Pallas kernels for 0%

profile of v1, /device:TPU:2, one launch (start us, length us, event | category | flops | bytes accessed | tf_op | source)
XLA Modules:
  0.0 793.5 jit_solution(12269404067772981891)
XLA Ops:
  54.0 38.9 %reduce-scatter.3.cloned.1.call-done = f32[128,192]{0,1:T(8,128)} async-done(((f32[1024,192]{0,1:T(8,128)}), f32[128,192]{0,1:T(8,128)}) %reduce-scatter.3.cloned.1.call-update) | async-done | bytes 98320 | tf_op jit(solution)/shard_map/reduce_scatter | solution.py:79
  104.8 261.0 %while.22 = (s32[]{:T(128)}, f32[128,1,4096]{2,1,0:T(1,128)}, s32[]{:T(128)}, s32[128]{0:T(128)S(1)}, s32[128,64]{1,0:T(8,128)S(1)}, /*index=5*/bf16[272,64,1,64...) while((s32[]{:T(128)}, f32[128,1,4096]{2,1,0:T(1,128)}, ...), condition=%wide.region_4.5_spmd.clone, body=%wide.region_3.4_spmd.clone.sunk | while | flops 8589834 | bytes 31015652 | solution.py:46
  105.0 9.9 %copy.78 = bf16[272,64,64]{2,1,0:T(8,128)(2,1)} copy(bf16[272,64,64]{0,2,1:T(8,128)(2,1)} %bitcast.90) | data formatting | bytes 4456448 | tf_op jit(solution)/shard_map
  114.9 15.7 %gather_fusion.1 = bf16[1024,64,64]{2,1,0:T(8,128)(2,1)} fusion(bf16[272,64,64]{2,1,0:T(8,128)(2,1)} %copy.78, s32[1024]{0:T(1024)S(1)} %broadcast_clamp_fusion.6), kind=kCustom, calls=%fused_computation.clone.clone.1 | custom fusion | bytes 16781312 | tf_op jit(solution)/shard_map/while/body/gather | solution.py:37
  142.3 9.9 %copy.78 = bf16[272,64,64]{2,1,0:T(8,128)(2,1)} copy(bf16[272,64,64]{0,2,1:T(8,128)(2,1)} %bitcast.90) | data formatting | bytes 4456448 | tf_op jit(solution)/shard_map
  152.1 15.7 %gather_fusion.1 = bf16[1024,64,64]{2,1,0:T(8,128)(2,1)} fusion(bf16[272,64,64]{2,1,0:T(8,128)(2,1)} %copy.78, s32[1024]{0:T(1024)S(1)} %broadcast_clamp_fusion.6), kind=kCustom, calls=%fused_computation.clone.clone.1 | custom fusion | bytes 16781312 | tf_op jit(solution)/shard_map/while/body/gather | solution.py:37
  179.6 9.9 %copy.78 = bf16[272,64,64]{2,1,0:T(8,128)(2,1)} copy(bf16[272,64,64]{0,2,1:T(8,128)(2,1)} %bitcast.90) | data formatting | bytes 4456448 | tf_op jit(solution)/shard_map
  189.4 15.7 %gather_fusion.1 = bf16[1024,64,64]{2,1,0:T(8,128)(2,1)} fusion(bf16[272,64,64]{2,1,0:T(8,128)(2,1)} %copy.78, s32[1024]{0:T(1024)S(1)} %broadcast_clamp_fusion.6), kind=kCustom, calls=%fused_computation.clone.clone.1 | custom fusion | bytes 16781312 | tf_op jit(solution)/shard_map/while/body/gather | solution.py:37
  216.9 9.9 %copy.78 = bf16[272,64,64]{2,1,0:T(8,128)(2,1)} copy(bf16[272,64,64]{0,2,1:T(8,128)(2,1)} %bitcast.90) | data formatting | bytes 4456448 | tf_op jit(solution)/shard_map
  226.7 15.7 %gather_fusion.1 = bf16[1024,64,64]{2,1,0:T(8,128)(2,1)} fusion(bf16[272,64,64]{2,1,0:T(8,128)(2,1)} %copy.78, s32[1024]{0:T(1024)S(1)} %broadcast_clamp_fusion.6), kind=kCustom, calls=%fused_computation.clone.clone.1 | custom fusion | bytes 16781312 | tf_op jit(solution)/shard_map/while/body/gather | solution.py:37
  264.0 15.7 %gather_fusion.1 = bf16[1024,64,64]{2,1,0:T(8,128)(2,1)} fusion(bf16[272,64,64]{2,1,0:T(8,128)(2,1)} %copy.78, s32[1024]{0:T(1024)S(1)} %broadcast_clamp_fusion.6), kind=kCustom, calls=%fused_computation.clone.clone.1 | custom fusion | bytes 16781312 | tf_op jit(solution)/shard_map/while/body/gather | solution.py:37
  301.3 15.7 %gather_fusion.1 = bf16[1024,64,64]{2,1,0:T(8,128)(2,1)} fusion(bf16[272,64,64]{2,1,0:T(8,128)(2,1)} %copy.78, s32[1024]{0:T(1024)S(1)} %broadcast_clamp_fusion.6), kind=kCustom, calls=%fused_computation.clone.clone.1 | custom fusion | bytes 16781312 | tf_op jit(solution)/shard_map/while/body/gather | solution.py:37
  328.7 9.9 %copy.78 = bf16[272,64,64]{2,1,0:T(8,128)(2,1)} copy(bf16[272,64,64]{0,2,1:T(8,128)(2,1)} %bitcast.90) | data formatting | bytes 4456448 | tf_op jit(solution)/shard_map
  338.5 15.7 %gather_fusion.1 = bf16[1024,64,64]{2,1,0:T(8,128)(2,1)} fusion(bf16[272,64,64]{2,1,0:T(8,128)(2,1)} %copy.78, s32[1024]{0:T(1024)S(1)} %broadcast_clamp_fusion.6), kind=kCustom, calls=%fused_computation.clone.clone.1 | custom fusion | bytes 16781312 | tf_op jit(solution)/shard_map/while/body/gather | solution.py:37
  373.6 232.7 %while.21 = (s32[]{:T(128)}, f32[128,1,64]{2,1,0:T(1,128)S(1)}, s32[]{:T(128)}, f32[128,1,4096]{2,1,0:T(1,128)}, f32[128,1]{0,1:T(1,128)S(1)}, /*index=5*/s32[12...) while((s32[]{:T(128)}, f32[128,1,64]{2,1,0:T(1,128)S(1)}, ...), condition=%wide.region_8.9_spmd, body=%wide.region_7.8_spmd.sunk | while | flops 8531978 | bytes 30765792 | solution.py:61
  383.0 15.7 %gather_fusion = bf16[1024,64,64]{2,1,0:T(8,128)(2,1)} fusion(bf16[272,64,64]{2,1,0:T(8,128)(2,1)} %copy.76, s32[1024]{0:T(1024)S(1)} %broadcast_clamp_fusion.5), kind=kCustom, calls=%fused_computation.1.clone.1 | custom fusion | bytes 16781312 | tf_op jit(solution)/shard_map/while/body/gather | solution.py:56
  416.2 15.7 %gather_fusion = bf16[1024,64,64]{2,1,0:T(8,128)(2,1)} fusion(bf16[272,64,64]{2,1,0:T(8,128)(2,1)} %copy.76, s32[1024]{0:T(1024)S(1)} %broadcast_clamp_fusion.5), kind=kCustom, calls=%fused_computation.1.clone.1 | custom fusion | bytes 16781312 | tf_op jit(solution)/shard_map/while/body/gather | solution.py:56
  449.5 15.7 %gather_fusion = bf16[1024,64,64]{2,1,0:T(8,128)(2,1)} fusion(bf16[272,64,64]{2,1,0:T(8,128)(2,1)} %copy.76, s32[1024]{0:T(1024)S(1)} %broadcast_clamp_fusion.5), kind=kCustom, calls=%fused_computation.1.clone.1 | custom fusion | bytes 16781312 | tf_op jit(solution)/shard_map/while/body/gather | solution.py:56
  482.7 15.7 %gather_fusion = bf16[1024,64,64]{2,1,0:T(8,128)(2,1)} fusion(bf16[272,64,64]{2,1,0:T(8,128)(2,1)} %copy.76, s32[1024]{0:T(1024)S(1)} %broadcast_clamp_fusion.5), kind=kCustom, calls=%fused_computation.1.clone.1 | custom fusion | bytes 16781312 | tf_op jit(solution)/shard_map/while/body/gather | solution.py:56
  516.0 15.7 %gather_fusion = bf16[1024,64,64]{2,1,0:T(8,128)(2,1)} fusion(bf16[272,64,64]{2,1,0:T(8,128)(2,1)} %copy.76, s32[1024]{0:T(1024)S(1)} %broadcast_clamp_fusion.5), kind=kCustom, calls=%fused_computation.1.clone.1 | custom fusion | bytes 16781312 | tf_op jit(solution)/shard_map/while/body/gather | solution.py:56
  549.2 15.7 %gather_fusion = bf16[1024,64,64]{2,1,0:T(8,128)(2,1)} fusion(bf16[272,64,64]{2,1,0:T(8,128)(2,1)} %copy.76, s32[1024]{0:T(1024)S(1)} %broadcast_clamp_fusion.5), kind=kCustom, calls=%fused_computation.1.clone.1 | custom fusion | bytes 16781312 | tf_op jit(solution)/shard_map/while/body/gather | solution.py:56
  582.4 15.7 %gather_fusion = bf16[1024,64,64]{2,1,0:T(8,128)(2,1)} fusion(bf16[272,64,64]{2,1,0:T(8,128)(2,1)} %copy.76, s32[1024]{0:T(1024)S(1)} %broadcast_clamp_fusion.5), kind=kCustom, calls=%fused_computation.1.clone.1 | custom fusion | bytes 16781312 | tf_op jit(solution)/shard_map/while/body/gather | solution.py:56
  607.2 92.9 %all-gather = bf16[1024,1,64]{0,2,1:T(8,128)(2,1)S(1)} all-gather(bf16[128,1,64]{0,2,1:T(8,128)(2,1)S(1)} %fusion.16), channel_id=2, replica_groups=mesh['row'=8,'col'=32] {'row'}, dimensions={0}, use_global_device_ids=true | all-gather | bytes 147456 | tf_op jit(solution)/shard_map/all_gather | solution.py:109
  704.7 81.9 %reduce-scatter.5.cloned.1.call-done = bf16[32,256]{1,0:T(8,128)(2,1)} async-done(((bf16[1024,256]{1,0:T(8,128)(2,1)}), bf16[32,256]{1,0:T(8,128)(2,1)}) %reduce-scatter.5.cloned.1.call-update) | async-done | bytes 16400 | tf_op jit(solution)/shard_map/reduce_scatter | solution.py:111
  (174 shorter events, 294.9 us)
Async XLA Ops:
  7.2 36.4 %copy-start = (bf16[256,192]{0,1:T(8,128)(2,1)S(1)}, bf16[256,192]{0,1:T(8,128)(2,1)}, u32[]{:S(2)}) copy-start(bf16[256,192]{0,1:T(8,128)(2,1)} %param.13) | copy-start | bytes 294916
  8.8 17.3 %all-to-all-start.1 = ((bf16[32,32,256]{2,1,0:T(8,128)(2,1)}), bf16[32,32,256]{2,1,0:T(8,128)(2,1)S(1)}, u32[]{:S(2)}, u32[]{:S(2)}) async-start(bf16[32,32,256]{2,1,0:T(8,128)(2,1)} %stack.2), calls=%async_computation.1 | async-start | bytes 1048576 | tf_op jit(solution)/shard_map/all_to_all | solution.py:76
  20.4 14.2 %copy-start.6 = (s32[1024]{0:T(1024)S(1)}, s32[1024]{0:T(1024)}, u32[]{:S(2)}) copy-start(s32[1024]{0:T(1024)} %param.19) | copy-start | bytes 12292
  26.1 67.7 %all-to-all-start = ((bf16[8,16,64,128]{3,2,1,0:T(8,128)(2,1)}), bf16[8,16,64,128]{3,2,1,0:T(8,128)(2,1)S(1)}, u32[]{:S(2)}, u32[]{:S(2)}) async-start(bf16[8,16,64,128]{3,2,1,0:T(8,128)(2,1)} %select_select_fusion), calls=%async_computation | async-start | bytes 4194304 | tf_op jit(solution)/shard_map/all_to_all | solution.py:100
  34.6 10.4 %copy-start.7 = (s32[128]{0:T(128)S(1)}, s32[128]{0:T(128)}, u32[]{:S(2)}) copy-start(s32[128]{0:T(128)} %param.17) | copy-start | bytes 1540
  34.6 58.2 %reduce-scatter.3.cloned.1.call-start = ((), (), s32[]{:S(2)}) async-start(), calls=%async_computation.4 | async-start | bytes 884736 | tf_op jit(solution)/shard_map/reduce_scatter | solution.py:79
  44.9 741.8 %reduce-scatter.5.cloned.1.call-start = ((), (), s32[]{:S(2)}) async-start(), calls=%async_computation.5 | async-start | bytes 540672 | tf_op jit(solution)/shard_map/reduce_scatter | solution.py:111
  46.2 6.9 copy-start.3
  94.4 4.4 copy-start.2
  373.5 326.8 %copy-start.5 = (s32[1024]{0:T(1024)S(1)}, s32[1024]{0:T(1024)}, u32[]{:S(2)}) copy-start(s32[1024]{0:T(1024)} %get-tuple-element.191) | copy-start | bytes 12292
  373.6 330.0 %copy-start.4 = (bf16[64,256]{1,0:T(8,128)(2,1)S(1)}, bf16[64,256]{1,0:T(8,128)(2,1)}, u32[]{:S(2)}) copy-start(bf16[64,256]{1,0:T(8,128)(2,1)} %param.14) | copy-start | bytes 98308
  373.6 330.0 %copy-start.8 = (pred[1024]{0:T(1024)(128)(4,1)S(1)}, pred[1024]{0:T(1024)(128)(4,1)}, u32[]{:S(2)}) copy-start(pred[1024]{0:T(1024)(128)(4,1)} %compare_and_fusion.1) | copy-start | bytes 3076
  606.3 180.3 %copy-start.1 = (bf16[256,192]{0,1:T(8,128)(2,1)S(1)}, bf16[256,192]{0,1:T(8,128)(2,1)}, u32[]{:S(2)}) copy-start(bf16[256,192]{0,1:T(8,128)(2,1)} %param.13) | copy-start | bytes 294916
Sparse Core Ops, SparseCore 0:
  45.0 47.7 reduce-scatter.2
  704.9 81.7 reduce-scatter.4
